TPU v7x, 512 devices: a whole 4x8x8 slice. The times are simulated.
512 devices in a mesh: sector: 8 (over z_hi, x), term: 64 (over y, z_lo, core).
Axes of the slice: x: 4, y: 8, z: 8 (z_hi: 2, z_lo: 4; z = z_hi * 4 + z_lo), core: 2. Of those that a mesh axis runs over, the one named last changes fastest.
Arguments:
- trial: bfloat16 [4096, 1024], P(('sector', 'term')), may hold values from -6 to 6
- block_rows: int32 [16], P('sector'), may hold values from 64 to 256, as said below
- right_ops: bfloat16 [512, 1024, 1024], P(('sector', 'term')), may hold values from -0.1875 to 0.1875
- left_ops: bfloat16 [512, 8, 256, 256], P(('sector', 'term')), may hold values from -0.046875 to 0.046875
- ent_source: int32 [512, 8], P(('sector', 'term')), may hold values from 0 to 3
- ent_target: int32 [512, 8], P(('sector', 'term')), may hold values from 0 to 1
- ent_count: int32 [512], P(('sector', 'term')), may hold values from 1 to 8, as said below
Outputs:
- sigma: bfloat16 [4096, 1024], P(('sector', 'term'))
Inputs may be any that keep to these rules, and one draw needn't show every extreme that they name: `block_rows`: some block has exactly 256 rows in every draw. Only entries k < ent_count[t] of term t are live; some term has 8 live entries in every draw.
All inputs are finite; a program needn't handle non-finite values.
Results may differ from a plain program's by a relative error of at most 0.005.
Values may be sent and summed in bfloat16 or wider, within the bound.
A program may use at most 64 MiB of HBM per device.

v0:
```python
import jax
import jax.numpy as jnp
from jax import lax
from jax.sharding import PartitionSpec as P


def passed_along(value, axis, steps):
    count = lax.axis_size(axis)
    initial, last = (max(0, -steps), min(count, count - steps))
    return lax.ppermute(value, axis, [(source, source + steps) for source in range(initial, last)])


def local(trial, block_rows, right_ops, left_ops, ent_source, ent_target, ent_count):
    rows_dev, columns = trial.shape
    block_len = left_ops.shape[2]
    group_blocks = block_rows.shape[0]
    offset = lax.axis_index("term") * rows_dev
    row_index = offset + jnp.arange(rows_dev, dtype=jnp.int32)
    owner_block = row_index // block_len
    inside = row_index % block_len
    limits = jnp.sum(
        jnp.where(
            owner_block[:, None] == jnp.arange(group_blocks, dtype=jnp.int32)[None, :],
            block_rows[None, :],
            0,
        ),
        axis=1,
    )
    live_rows = inside < limits
    masked = jnp.where(live_rows[:, None], trial, jnp.zeros_like(trial))
    operator = right_ops[0]
    gathered = lax.all_gather(masked, "term", axis=0, tiled=True)
    previous = passed_along(gathered, "sector", 1)
    window = jnp.concatenate([gathered, previous], 0)
    projected = jnp.dot(window, operator, preferred_element_type=jnp.float32).astype(jnp.bfloat16)
    sources = projected.reshape(2 * group_blocks, block_len, columns)
    lefts = left_ops[0]
    source_ids = ent_source[0]
    target_ids = ent_target[0]
    live_count = ent_count[0]

    def add_entry(slot, totals):
        one_block = lax.dynamic_index_in_dim(sources, source_ids[slot], 0, keepdims=False)
        left_op = lax.dynamic_index_in_dim(lefts, slot, 0, keepdims=False)
        product = jnp.dot(left_op, one_block, preferred_element_type=jnp.float32)
        current = lax.dynamic_index_in_dim(totals, target_ids[slot], 0, keepdims=False)
        return lax.dynamic_update_index_in_dim(totals, current + product, target_ids[slot], 0)

    start = jnp.zeros((group_blocks, block_len, columns), jnp.float32)
    totals = lax.fori_loop(0, live_count, add_entry, start)
    partial_value = totals.reshape(group_blocks * block_len, columns)
    own_rows = lax.psum_scatter(partial_value, "term", scatter_dimension=0, tiled=True)
    return jnp.where(live_rows[:, None], own_rows, 0.0).astype(jnp.bfloat16)


def solution(mesh):
    placed = (
        P(("sector", "term"), None),
        P("sector"),
        P(("sector", "term"), None, None),
        P(("sector", "term"), None, None, None),
        P(("sector", "term"), None),
        P(("sector", "term"), None),
        P(("sector", "term")),
    )
    return jax.shard_map(
        local, mesh=mesh, in_specs=placed, out_specs=P(("sector", "term"), None), check_vma=False
    )
```

profile of v0, /device:TPU:6, one launch (start us, length us, event | category | flops | bytes accessed | tf_op | source)
XLA Modules:
  0.0 559.6 jit_solution(2002737886397981179)
XLA Ops:
  6.5 0.0 copy-start
  6.5 0.0 all-gather.2.cloned.1.call-start
  6.6 0.9 fusion.17
  7.5 1.4 broadcast_select_fusion
  8.9 0.0 all-gather.2.cloned.1.call-update
  8.9 0.0 reduce-scatter.2.cloned.1.call-start
  8.9 122.3 %all-gather.2.cloned.1.call-done = bf16[512,1024]{1,0:T(8,128)(2,1)} async-done(((bf16[8,1024]{1,0:T(8,128)(2,1)}), bf16[512,1024]{1,0:T(8,128)(2,1)}) %all-gather.2.cloned.1.call-update) | async-done | bytes 1048592 | tf_op jit(solution)/shard_map/all_gather | solution.py:32
  131.2 5.8 %collective-permute-start = (bf16[512,1024]{1,0:T(8,128)(2,1)}, bf16[512,1024]{1,0:T(8,128)(2,1)S(1)}, u32[]{:S(2)}, u32[]{:S(2)}) collective-permute-start(bf16[512,1024]{1,0:T(8,128)(2,1)} %all-gather.2.cloned.1.call-done), channel_id=1, source_target_pairs={{0,64},{64,128},{128,192},{192,256},{256,320},{320,384},{384,448},... | collective-permute-start | bytes 3145736 | tf_op jit(solution)/shard_map/ppermute | solution.py:10
  137.0 23.1 %collective-permute-done = bf16[512,1024]{1,0:T(8,128)(2,1)S(1)} collective-permute-done((bf16[512,1024]{1,0:T(8,128)(2,1)}, bf16[512,1024]{1,0:T(8,128)(2,1)S(1)}, u32[]{:S(2)}, u32[]{:S(2)}) %collective-permute-start) | collective-permute-done | bytes 1048608 | tf_op jit(solution)/shard_map/ppermute | solution.py:10
  160.1 0.0 copy-done
  160.1 4.9 fusion.12
  165.0 1.6 broadcast_in_dim.48
  166.6 0.0 copy-done.3
  166.6 0.0 copy-done.4
  166.6 10.8 %while.10 = (s32[]{:T(128)}, f32[2,256,1024]{2,1,0:T(8,128)}, s32[]{:T(128)}, s32[8]{0:T(128)S(1)}, bf16[8,256,256]{2,1,0:T(8,128)(2,1)}, /*index=5*/s32[8]{0:T(...) while((s32[]{:T(128)}, f32[2,256,1024]{2,1,0:T(8,128)}, ...), condition=%wide.region_2.3_spmd, body=%wide.region_1.2_spmd.sunk | while | flops 134479888 | bytes 21627204 | solution.py:50
  167.3 0.6 dynamic_slice.36
  169.7 0.6 dynamic_slice.37
  172.2 1.5 constant_dynamic-slice_fusion.2
  173.7 0.4 copy-done.1
  174.1 1.4 fusion.25
  175.5 1.3 copy-done.2
  177.5 0.0 reduce-scatter.2.cloned.1.call-update
  177.5 373.8 %reduce-scatter.2.cloned.1.call-done = f32[8,1024]{1,0:T(8,128)} async-done(((f32[512,1024]{1,0:T(8,128)}), f32[8,1024]{1,0:T(8,128)}) %reduce-scatter.2.cloned.1.call-update) | async-done | bytes 32784 | tf_op jit(solution)/shard_map/reduce_scatter | solution.py:52
  551.3 1.4 select_convert_fusion
  (6 shorter events, 0.0 us)
Async XLA Ops:
  6.5 153.6 %copy-start = (bf16[1,1024,1024]{2,1,0:T(8,128)(2,1)S(1)}, bf16[1,1024,1024]{2,1,0:T(8,128)(2,1)}, u32[]{:S(2)}) copy-start(bf16[1,1024,1024]{2,1,0:T(8,128)(2,1)} %param.11) | copy-start | bytes 6291460
  6.5 124.6 %all-gather.2.cloned.1.call-start = ((), (), s32[]{:S(2)}) async-start(), calls=%async_computation.1 | async-start | bytes 1064960 | tf_op jit(solution)/shard_map/all_gather | solution.py:32
  8.9 542.5 %reduce-scatter.2.cloned.1.call-start = ((), (), s32[]{:S(2)}) async-start(), calls=%async_computation.2 | async-start | bytes 2129920 | tf_op jit(solution)/shard_map/reduce_scatter | solution.py:52
  131.2 28.9 %collective-permute-start = (bf16[512,1024]{1,0:T(8,128)(2,1)}, bf16[512,1024]{1,0:T(8,128)(2,1)S(1)}, u32[]{:S(2)}, u32[]{:S(2)}) collective-permute-start(bf16[512,1024]{1,0:T(8,128)(2,1)} %all-gather.2.cloned.1.call-done), channel_id=1, source_target_pairs={{0,64},{64,128},{128,192},{192,256},{256,320},{320,384},{384,448},... | collective-permute-start | bytes 3145736 | tf_op jit(solution)/shard_map/ppermute | solution.py:10
  165.0 1.6 copy-start.3
  165.0 1.6 copy-start.4
  172.2 1.9 copy-start.1
  175.5 1.3 copy-start.2
Sparse Core Ops, SparseCore 0:
  9.5 121.6 all-gather.1
  177.6 373.6 reduce-scatter.1
where the time goes:
time: 561 us; the launch traced here: 560 us
  waiting for transfers between devices  519 us (93%)
  between operations  13.4 us (2%)
  matrix products  6.32 us (1%)
  local copies, waits for them, and re-layouts  6.01 us (1%)
  starting transfers between devices  5.87 us (1%)
    reduce_scatter x1, waiting for transfers between devices, local(): lax.psum_scatter(partial_value, 'term', scatter_dimension=0, tiled=True)  374 us
    all_gather x1, waiting for transfers between devices, local(): gathered = lax.all_gather(masked, 'term', axis=0, tiled=True)  122 us
    ppermute x1, waiting for transfers between devices, passed_along(): lax.ppermute(value, axis, [(source, source + steps) for source in range(i...  23.1 us
  transfers between devices with their start and end apart: 3, of which 3 were waited for; matrix products, arithmetic and copies ran while one was open for 0% of the time, Pallas kernels for 0%

commit v1 on v0

v1 whole, which is shorter than its diff:
```python
import functools

import jax
import jax.numpy as jnp
from jax import lax
from jax.experimental import pallas as pl
from jax.experimental.pallas import tpu as pltpu
from jax.sharding import PartitionSpec as P

MESH = pl.DeviceIdType.MESH
F32 = jnp.float32
BF16 = jnp.bfloat16


def kernel(
    sectors, ny, nz,
    trial_ref, rows_ref, right_ref, left_ref, source_ref, target_ref, count_ref,
    out_ref,
    units, window, lefts, weights, weights_sib, right_own, right_sib, projected, outgoing, incoming,
    load_sem, pair_send, pair_recv, next_send, next_recv, z_send, z_recv, y_send, y_recv,
    d_send, d_recv, r_send, r_recv,
):
    entries, block_len = lefts.shape[0], lefts.shape[1]
    columns = right_own.shape[0]
    half = columns // 2
    group_rows = 2 * block_len
    chips = ny * nz
    far = ny // 2
    s = lax.axis_index("sector")
    t = lax.axis_index("term")
    y, z, c = t // (2 * nz), lax.rem(t // 2, nz), lax.rem(t, 2)
    me = t // 2

    def device(sector, chip, core):
        return (sector, chip * 2 + core)

    sibling = device(s, me, 1 - c)
    following = device(lax.rem(s + 1, sectors), me, c)
    preceding = device(lax.rem(s + sectors - 1, sectors), me, c)

    load_left = pltpu.make_async_copy(left_ref.at[0], lefts, load_sem.at[0])
    load_right = pltpu.make_async_copy(right_ref.at[0], right_own, load_sem.at[1])
    load_left.start()
    load_right.start()

    barrier = pltpu.get_barrier_semaphore()

    def greet(j, carry):
        chip = lax.rem(me + j, chips)
        pl.semaphore_signal(barrier, inc=1, device_id=device(s, chip, c), device_id_type=MESH)
        return carry

    pl.semaphore_signal(barrier, inc=1, device_id=sibling, device_id_type=MESH)
    pl.semaphore_signal(barrier, inc=1, device_id=preceding, device_id_type=MESH)
    lax.fori_loop(1, chips, greet, 0)

    start_row = t * 8
    limit = rows_ref[start_row // block_len]
    inside = lax.rem(start_row, block_len) + lax.broadcasted_iota(jnp.int32, (8, columns), 0)
    live_rows = inside < limit
    own = jnp.where(live_rows, trial_ref[...].astype(F32), 0.0)
    own = jnp.concatenate([own[:, :half], own[:, half:]], axis=0)
    units[0, c, y, z] = own.astype(BF16)

    load_left.wait()
    count = count_ref[0]
    factors = []
    for k in range(entries):
        live = k < count
        src, dst = source_ref[0, k], target_ref[0, k]
        for b in range(2):
            for w in range(4):
                on = live & (dst == b) & (src == w)
                if w >= 2:
                    on = on & (s > 0)
                factors.append(jnp.where(on, 1.0, 0.0).astype(F32))

    def weigh(i, carry):
        row = pl.multiple_of(i * 32, 32)
        blocks = [lefts[k, pl.ds(row, 32), :].astype(F32) for k in range(entries)]
        at = pl.multiple_of(i * 16, 16)
        for b in range(2):
            for w in range(4):
                total = blocks[0] * factors[b * 4 + w]
                for k in range(1, entries):
                    total = total + blocks[k] * factors[k * 8 + b * 4 + w]
                total = total.reshape(2, 2, 8, block_len)
                for p in range(2):
                    piece = total[:, p].reshape(16, block_len).astype(BF16)
                    weights[p, pl.ds(b * (block_len // 2) + at, 16), w * block_len:(w + 1) * block_len] = piece
        return carry

    lax.fori_loop(0, block_len // 32, weigh, 0)

    pl.semaphore_wait(barrier, chips - 1 + 2)

    def remote(source, destination, send, recv, target):
        return pltpu.make_async_remote_copy(
            src_ref=source, dst_ref=destination, send_sem=send, recv_sem=recv,
            device_id=target, device_id_type=MESH,
        )

    sends = []

    def begin(copy):
        copy.start()
        sends.append(copy)
        return copy

    def z_copies(st):
        slot = units.at[st, c, y, z]
        return [
            remote(slot, slot, z_send.at[st, d - 1], z_recv.at[st, d - 1],
                   device(s, y * nz + lax.rem(z + d, nz), c))
            for d in range(1, nz)
        ]

    def slab(st, way, k):
        row = lax.rem(y - k + ny, ny) if way == 0 else lax.rem(y + k, ny)
        if k < far:
            return units.at[st, c, row]
        return units.at[st, c, row, pl.ds(way * (nz // 2), nz // 2)]

    def y_copy(st, way, k):
        row = lax.rem(y - (k - 1) + ny, ny) if way == 0 else lax.rem(y + (k - 1), ny)
        if k < far:
            slot = units.at[st, c, row]
        else:
            slot = units.at[st, c, row, pl.ds(way * (nz // 2), nz // 2)]
        to = lax.rem(y + 1, ny) if way == 0 else lax.rem(y + ny - 1, ny)
        return remote(slot, slot, y_send.at[st, way, k - 1], y_recv.at[st, way, k - 1],
                      device(s, to * nz + z, c))

    def d_copy(st, way, k):
        index = 0 if k == 0 else way * far + k
        slot = units.at[st, c, y] if k == 0 else slab(st, way, k)
        return remote(slot, slot, d_send.at[st, index], d_recv.at[st, index], sibling)

    z_all = [z_copies(st) for st in range(2)]
    for copy in z_all[0]:
        begin(copy)
    next_copy = begin(remote(units.at[0, c, y, z], units.at[1, c, y, z], next_send.at[0], next_recv.at[0], following))
    weights_copy = begin(remote(weights.at[1 - c], weights_sib, pair_send.at[0], pair_recv.at[0], sibling))
    right_copy = begin(remote(right_ref.at[0], right_sib, pair_send.at[1], pair_recv.at[1], sibling))

    steps = {}
    pairs = []

    def begin_y(st, way, k):
        steps[st, way, k] = begin(y_copy(st, way, k))

    def begin_d(st, way, k):
        pairs.append((st, begin(d_copy(st, way, k))))

    for st in range(2):
        if st == 1:
            next_copy.wait_recv()
            for copy in z_all[1]:
                begin(copy)
        for copy in z_all[st]:
            copy.wait_recv()
        begin_y(st, 0, 1)
        begin_y(st, 1, 1)
        begin_d(st, 0, 0)
    for k in range(1, far + 1):
        for st in range(2):
            for way in range(2):
                steps[st, way, k].wait_recv()
                if k < far:
                    begin_y(st, way, k + 1)
                begin_d(st, way, k)

    def lay(st):
        def one(row, carry):
            pieces = [units[st, p, row].astype(F32).reshape(nz, 2, 8, half) for p in range(2)]
            at = pl.multiple_of(st * group_rows + row * (nz * 16), 16)
            for h in range(2):
                both = jnp.concatenate([pieces[0][:, h:h + 1], pieces[1][:, h:h + 1]], axis=1)
                window[pl.ds(at, nz * 16), h * half:(h + 1) * half] = both.reshape(nz * 16, half).astype(BF16)
            return carry

        lax.fori_loop(0, ny, one, 0)

    for st in range(2):
        for which, copy in pairs:
            if which == st:
                copy.wait_recv()
        lay(st)

    weights_copy.wait_recv()
    right_copy.wait_recv()
    load_right.wait()
    tile = min(256, half)
    for n in range(columns // tile):
        part = window[:, n * tile:(n + 1) * tile]
        projected[:, n * tile:(n + 1) * tile] = jnp.dot(
            weights[c], part, preferred_element_type=F32).astype(BF16)
        projected[:, columns + n * tile:columns + (n + 1) * tile] = jnp.dot(
            weights_sib[...], part, preferred_element_type=F32).astype(BF16)

    for n in range(half // tile):
        both = []
        for h in range(2):
            at = h * half + n * tile
            value = jnp.dot(projected[:, :columns], right_own[:, at:at + tile], preferred_element_type=F32)
            value = value + jnp.dot(projected[:, columns:], right_sib[:, at:at + tile], preferred_element_type=F32)
            both.append(value.reshape(chips, 8, tile))
        outgoing[:, :, n * tile:(n + 1) * tile] = jnp.concatenate(both, axis=1).astype(BF16)

    def scatter_copy(chip):
        return remote(outgoing.at[chip], incoming.at[me], r_send.at[chip], r_recv.at[me], device(s, chip, c))

    def scatter(j, carry):
        scatter_copy(lax.rem(me + j, chips)).start()
        return carry

    order = [far]
    for k in range(far - 1, -1, -1):
        order += [k, ny - k] if k else [0]
    for dy in order:
        row = lax.rem(y + dy, ny)
        for dz in range(nz - 1, -1, -1):
            if dy or dz:
                scatter_copy(row * nz + lax.rem(z + dz, nz)).start()
    incoming[me] = outgoing[me]

    def gathered(j, carry):
        chip = lax.rem(me + j, chips)
        remote(outgoing.at[chip], incoming.at[chip], r_send.at[chip], r_recv.at[chip], device(s, chip, c)).wait_recv()
        return carry

    lax.fori_loop(1, chips, gathered, 0)
    total = incoming[0].astype(F32)
    for chip in range(1, chips):
        total = total + incoming[chip].astype(F32)
    result = jnp.concatenate([total[0:8], total[8:16]], axis=1)
    out_ref[...] = jnp.where(live_rows, result, 0.0).astype(BF16)

    for copy in sends:
        copy.wait_send()

    def sent(j, carry):
        chip = lax.rem(me + j, chips)
        remote(outgoing.at[chip], incoming.at[chip], r_send.at[chip], r_recv.at[chip], device(s, chip, c)).wait_send()
        return carry

    lax.fori_loop(1, chips, sent, 0)


def local(sectors, ny, nz, trial, block_rows, right_ops, left_ops, ent_source, ent_target, ent_count):
    entries, block_len = left_ops.shape[1:3]
    columns = trial.shape[1]
    chips = ny * nz
    far = ny // 2
    dma = pltpu.SemaphoreType.DMA
    vmem = pl.BlockSpec(memory_space=pltpu.VMEM)
    smem = pl.BlockSpec(memory_space=pltpu.SMEM)
    hbm = pl.BlockSpec(memory_space=pl.ANY)
    return pl.pallas_call(
        functools.partial(kernel, sectors, ny, nz),
        out_shape=jax.ShapeDtypeStruct(trial.shape, trial.dtype),
        in_specs=[vmem, smem, hbm, hbm, smem, smem, smem],
        out_specs=vmem,
        scratch_shapes=[
            pltpu.VMEM((2, 2, ny, nz, 16, columns // 2), BF16),
            pltpu.VMEM((4 * block_len, columns), BF16),
            pltpu.VMEM((entries, block_len, block_len), BF16),
            pltpu.VMEM((2, block_len, 4 * block_len), BF16),
            pltpu.VMEM((block_len, 4 * block_len), BF16),
            pltpu.VMEM((columns, columns), BF16),
            pltpu.VMEM((columns, columns), BF16),
            pltpu.VMEM((block_len, 2 * columns), BF16),
            pltpu.VMEM((chips, 16, columns // 2), BF16),
            pltpu.VMEM((chips, 16, columns // 2), BF16),
            dma((2,)), dma((2,)), dma((2,)), dma((1,)), dma((1,)),
            dma((2, nz - 1)), dma((2, nz - 1)),
            dma((2, 2, far)), dma((2, 2, far)),
            dma((2, 2 * far + 1)), dma((2, 2 * far + 1)),
            dma((chips,)), dma((chips,)),
        ],
        compiler_params=pltpu.CompilerParams(
            collective_id=0, has_side_effects=True, vmem_limit_bytes=48 * 1024 * 1024,
        ),
        name="sigma",
    )(trial, block_rows, right_ops, left_ops, ent_source, ent_target, ent_count)


def solution(mesh):
    nz = 4
    sectors = mesh.shape["sector"]
    ny = mesh.shape["term"] // (2 * nz)
    placed = (
        P(("sector", "term"), None),
        P("sector"),
        P(("sector", "term"), None, None),
        P(("sector", "term"), None, None, None),
        P(("sector", "term"), None),
        P(("sector", "term"), None),
        P(("sector", "term")),
    )
    return jax.shard_map(
        functools.partial(local, sectors, ny, nz), mesh=mesh, in_specs=placed,
        out_specs=P(("sector", "term"), None), check_vma=False,
    )
```

time: 561 us -> 70.3 us (0.13)
  the two profiles are of different devices: /device:TPU:6 before, /device:TPU:1 now
where the time goes in v1:
time: 70.3 us; the launch traced here: 70 us
  Pallas kernels  63.3 us (90%)
  local copies, waits for them, and re-layouts  6.1 us (9%)
    pallas_call x1, Pallas kernels, local(): pl.pallas_call(functools.partial(kernel, sectors, ny, nz), out_shape=jax....  63.3 us
    unnamed x13, local copies, waits for them, and re-layouts  6.1 us

profile of v1, /device:TPU:1, one launch (start us, length us, event | category | flops | bytes accessed | tf_op | source)
XLA Modules:
  0.0 70.0 jit_solution(5862197285568944662)
XLA Ops:
  0.7 0.0 copy-start
  0.7 1.6 %copy-done = bf16[1,1024,1024]{2,1,0:T(8,128)(2,1)S(1)} copy-done((bf16[1,1024,1024]{2,1,0:T(8,128)(2,1)S(1)}, bf16[1,1024,1024]{2,1,0:T(8,128)(2,1)}, u32[]{:S(2)}) %copy-start) | copy-done | bytes 2097176
  2.2 0.0 copy-start.1
  2.2 1.2 %copy-done.1 = bf16[1,8,256,256]{3,2,1,0:T(8,128)(2,1)S(1)} copy-done((bf16[1,8,256,256]{3,2,1,0:T(8,128)(2,1)S(1)}, bf16[1,8,256,256]{3,2,1,0:T(8,128)(2,1)}, u32[]{:S(2)}) %copy-start.1) | copy-done | bytes 1048600
  3.5 0.0 copy-start.2
  3.5 0.7 %copy-done.2 = bf16[8,1024]{1,0:T(8,128)(2,1)S(1)} copy-done((bf16[8,1024]{1,0:T(8,128)(2,1)S(1)}, bf16[8,1024]{1,0:T(8,128)(2,1)}, u32[]{:S(2)}) %copy-start.2) | copy-done | bytes 16408
  4.2 0.0 copy-start.3
  4.2 0.7 copy-done.3
  4.8 0.0 copy-start.4
  4.8 0.7 copy-done.4
  5.5 0.0 copy-start.5
  5.5 0.7 copy-done.5
  6.2 63.3 %sigma.1 = bf16[8,1024]{1,0:T(8,128)(2,1)S(1)} custom-call(bf16[8,1024]{1,0:T(8,128)(2,1)S(1)} %copy-done.2, s32[2]{0:T(128)S(1)} %copy-done.3, bf16[1,1024,1024]{2,1,0:T(8,128)(2,1)S(1)} %copy-done, bf16[1,8,256,256]{3,2,1,0:T(8,128)(2,1)S(1)} %copy-done.1, s32[1,8]{1,0:T(1,128)S(1)} %copy-done.4, s32[1,8]{1,0:T(1,128)S(1)} %copy-done.5, s32[1]{0:T(128)S(6)} %copy.9.count_ref), custom_call_target="tpu_custom_call" | custom-call | tf_op jit(solution)/shard_map/sigma/pallas_call | solution.py:259
  69.4 0.6 copy.10
Async XLA Ops:
  0.7 1.6 %copy-start = (bf16[1,1024,1024]{2,1,0:T(8,128)(2,1)S(1)}, bf16[1,1024,1024]{2,1,0:T(8,128)(2,1)}, u32[]{:S(2)}) copy-start(bf16[1,1024,1024]{2,1,0:T(8,128)(2,1)} %right_ref.1) | copy-start | bytes 6291460
  2.2 1.2 %copy-start.1 = (bf16[1,8,256,256]{3,2,1,0:T(8,128)(2,1)S(1)}, bf16[1,8,256,256]{3,2,1,0:T(8,128)(2,1)}, u32[]{:S(2)}) copy-start(bf16[1,8,256,256]{3,2,1,0:T(8,128)(2,1)} %left_ref.1) | copy-start | bytes 3145732
  3.5 0.7 %copy-start.2 = (bf16[8,1024]{1,0:T(8,128)(2,1)S(1)}, bf16[8,1024]{1,0:T(8,128)(2,1)}, u32[]{:S(2)}) copy-start(bf16[8,1024]{1,0:T(8,128)(2,1)} %trial_ref.1) | copy-start | bytes 49156
  4.2 0.7 copy-start.3
  4.8 0.7 copy-start.4
  5.5 0.7 copy-start.5

commit v2 on v1

v2 whole, which is shorter than its diff:
```python
import functools

import jax
import jax.numpy as jnp
from jax import lax
from jax.experimental import pallas as pl
from jax.experimental.pallas import tpu as pltpu
from jax.sharding import PartitionSpec as P

MESH = pl.DeviceIdType.MESH
F32 = jnp.float32
BF16 = jnp.bfloat16


def kernel(
    sectors, ny, nz,
    trial_in, rows_in, right_ref, left_ref, source_in, target_in, count_in,
    out_ref,
    trial_ref, rows_ref, source_ref, target_ref, count_ref,
    units, window, lefts, weights, weights_sib, right_own, right_sib, projected, outgoing, incoming,
    passed, passed_half,
    load_sem, pair_send, pair_recv, next_send, next_recv, z_send, z_recv, y_send, y_recv,
    d_send, d_recv, m_send, m_recv, r_send, r_recv,
):
    entries, block_len = lefts.shape[0], lefts.shape[1]
    columns = right_own.shape[0]
    half = columns // 2
    group_rows = 2 * block_len
    chips = ny * nz
    far = ny // 2
    s = lax.axis_index("sector")
    t = lax.axis_index("term")
    y, z, c = t // (2 * nz), lax.rem(t // 2, nz), lax.rem(t, 2)
    me = t // 2

    def device(sector, chip, core):
        return (sector, chip * 2 + core)

    sibling = device(s, me, 1 - c)
    following = lax.rem(s + 1, sectors)
    preceding = lax.rem(s + sectors - 1, sectors)

    def near(dy, dz):
        return lax.rem(y + dy + ny, ny) * nz + lax.rem(z + dz, nz)


    loads = [
        pltpu.make_async_copy(source, destination, load_sem.at[i])
        for i, (source, destination) in enumerate([
            (trial_in, trial_ref), (rows_in, rows_ref), (source_in, source_ref), (target_in, target_ref),
            (count_in, count_ref), (left_ref.at[0], lefts), (right_ref.at[0], right_own),
        ])
    ]
    for load in loads:
        load.start()

    barrier = pltpu.get_barrier_semaphore()

    def greet(target):
        pl.semaphore_signal(barrier, inc=1, device_id=target, device_id_type=MESH)

    greet(sibling)
    for dz in range(nz):
        greet(device(preceding, near(0, dz), c))
    for dy in range(-2, 3):
        for dz in range(nz):
            if dy or dz:
                greet(device(s, near(dy, dz), c))

    loads[0].wait()
    loads[1].wait()
    start_row = t * 8
    limit = rows_ref[start_row // block_len]
    inside = lax.rem(start_row, block_len) + lax.broadcasted_iota(jnp.int32, (8, columns), 0)
    live_rows = inside < limit
    own = jnp.where(live_rows, trial_ref[...].astype(F32), 0.0)
    own = jnp.concatenate([own[:, :half], own[:, half:]], axis=0)
    units[0, c, y, z] = own.astype(BF16)

    pl.semaphore_wait(barrier, 1 + nz + 5 * nz - 1)

    def remote(source, destination, send, recv, target):
        return pltpu.make_async_remote_copy(
            src_ref=source, dst_ref=destination, send_sem=send, recv_sem=recv,
            device_id=target, device_id_type=MESH,
        )

    sends = []

    def begin(copy):
        copy.start()
        sends.append(copy)
        return copy

    def z_copies():
        slot = units.at[0, c, y, z]
        return [
            remote(slot, slot, z_send.at[d - 1], z_recv.at[d - 1], device(s, near(0, d), c))
            for d in range(1, nz)
        ]

    def slab(st, way, k):
        row = lax.rem(y - k + ny, ny) if way == 0 else lax.rem(y + k, ny)
        if k < far:
            return units.at[st, c, row]
        return units.at[st, c, row, pl.ds(way * (nz // 2), nz // 2)]

    def y_copy(st, way, k):
        row = lax.rem(y - (k - 1) + ny, ny) if way == 0 else lax.rem(y + (k - 1), ny)
        if k < far:
            slot = units.at[st, c, row]
        else:
            slot = units.at[st, c, row, pl.ds(way * (nz // 2), nz // 2)]
        to = lax.rem(y + 1, ny) if way == 0 else lax.rem(y + ny - 1, ny)
        return remote(slot, slot, y_send.at[st, way, k - 1], y_recv.at[st, way, k - 1],
                      device(s, to * nz + z, c))

    def d_copy(st, way, k):
        index = 0 if k == 0 else way * far + k
        slot = units.at[st, c, y] if k == 0 else slab(st, way, k)
        return remote(slot, slot, d_send.at[st, index], d_recv.at[st, index], sibling)

    z_all = [begin(copy) for copy in z_copies()]
    next_all = [
        begin(remote(units.at[0, c, y, z], units.at[1, c, y, z], next_send.at[d], next_recv.at[d],
                     device(following, near(0, d), c)))
        for d in range(nz)
    ]
    right_copy = begin(remote(right_ref.at[0], right_sib, pair_send.at[1], pair_recv.at[1], sibling))

    for load in loads[2:6]:
        load.wait()
    count = count_ref[0, 0]
    factors = []
    for k in range(entries):
        live = k < count
        src, dst = source_ref[0, k], target_ref[0, k]
        for b in range(2):
            for w in range(4):
                on = live & (dst == b) & (src == w)
                if w >= 2:
                    on = on & (s > 0)
                factors.append(jnp.where(on, 1.0, 0.0).astype(F32))

    def weigh(i, carry):
        row = pl.multiple_of(i * 32, 32)
        blocks = [lefts[k, pl.ds(row, 32), :].astype(F32) for k in range(entries)]
        at = pl.multiple_of(i * 16, 16)
        for b in range(2):
            for w in range(4):
                total = blocks[0] * factors[b * 4 + w]
                for k in range(1, entries):
                    total = total + blocks[k] * factors[k * 8 + b * 4 + w]
                total = total.reshape(2, 2, 8, block_len)
                for p in range(2):
                    piece = total[:, p].reshape(16, block_len).astype(BF16)
                    weights[p, pl.ds(b * (block_len // 2) + at, 16), w * block_len:(w + 1) * block_len] = piece
        return carry

    lax.fori_loop(0, block_len // 32, weigh, 0)

    weights_copy = begin(remote(weights.at[1 - c], weights_sib, pair_send.at[0], pair_recv.at[0], sibling))

    steps = {}
    pairs = []

    def begin_y(st, way, k):
        steps[st, way, k] = begin(y_copy(st, way, k))

    def begin_d(st, way, k):
        pairs.append((st, begin(d_copy(st, way, k))))

    for st in range(2):
        for copy in (next_all if st else z_all):
            copy.wait_recv()
        begin_y(st, 0, 1)
        begin_y(st, 1, 1)
        begin_d(st, 0, 0)
    for k in range(1, far + 1):
        for st in range(2):
            for way in range(2):
                steps[st, way, k].wait_recv()
                if k < far:
                    begin_y(st, way, k + 1)
                begin_d(st, way, k)

    def lay(st):
        def one(row, carry):
            pieces = [units[st, p, row].astype(F32).reshape(nz, 2, 8, half) for p in range(2)]
            at = pl.multiple_of(st * group_rows + row * (nz * 16), 16)
            for h in range(2):
                both = jnp.concatenate([pieces[0][:, h:h + 1], pieces[1][:, h:h + 1]], axis=1)
                window[pl.ds(at, nz * 16), h * half:(h + 1) * half] = both.reshape(nz * 16, half).astype(BF16)
            return carry

        lax.fori_loop(0, ny, one, 0)

    for st in range(2):
        for which, copy in pairs:
            if which == st:
                copy.wait_recv()
        lay(st)

    weights_copy.wait_recv()
    right_copy.wait_recv()
    loads[6].wait()
    tile = min(256, half)
    for n in range(columns // tile):
        part = window[:, n * tile:(n + 1) * tile]
        projected[:, n * tile:(n + 1) * tile] = jnp.dot(
            weights[c], part, preferred_element_type=F32).astype(BF16)
        projected[:, columns + n * tile:columns + (n + 1) * tile] = jnp.dot(
            weights_sib[...], part, preferred_element_type=F32).astype(BF16)

    for n in range(half // tile):
        both = []
        for h in range(2):
            at = h * half + n * tile
            value = jnp.dot(projected[:, :columns], right_own[:, at:at + tile], preferred_element_type=F32)
            value = value + jnp.dot(projected[:, columns:], right_sib[:, at:at + tile], preferred_element_type=F32)
            both.append(value.reshape(chips, 8, tile))
        outgoing[:, :, n * tile:(n + 1) * tile] = jnp.concatenate(both, axis=1).astype(BF16)

    def row_at(dy):
        return lax.rem(y + dy + ny, ny) * nz

    merged = []
    for way, sign in ((0, 1), (1, -1)):
        merged.append((
            begin(remote(outgoing.at[pl.ds(row_at(3 * sign), nz)], passed.at[way],
                         m_send.at[way, 0], m_recv.at[way, 0], device(s, near(sign, 0), c))),
            begin(remote(outgoing.at[pl.ds(row_at(4) + way * (nz // 2), nz // 2)], passed_half.at[way],
                         m_send.at[way, 1], m_recv.at[way, 1], device(s, near(2 * sign, 0), c))),
        ))

    finals = []

    def deliver(dy, dz):
        chip = near(dy, dz)
        finals.append(begin(remote(
            outgoing.at[chip], incoming.at[(2 + dy) * nz + z],
            r_send.at[(2 + dy) * nz + dz], r_recv.at[(2 + dy) * nz + dz], device(s, chip, c))))

    for dy in (1, -1, 0):
        for dz in range(nz - 1, -1, -1):
            if dy or dz:
                deliver(dy, dz)
    incoming[2 * nz + z] = outgoing[me]
    for way, sign in ((0, 1), (1, -1)):
        whole, part = merged[way]
        whole.wait_recv()
        part.wait_recv()
        for i in range(nz):
            at = row_at(2 * sign) + i
            value = outgoing[at].astype(F32) + passed[way, i].astype(F32)
            if i // (nz // 2) == way:
                value = value + passed_half[way, i % (nz // 2)].astype(F32)
            outgoing[at] = value.astype(BF16)
        for dz in range(nz - 1, -1, -1):
            deliver(2 * sign, dz)

    for copy in finals:
        copy.wait_recv()
    total = incoming[0].astype(F32)
    for i in range(1, 5 * nz):
        total = total + incoming[i].astype(F32)
    result = jnp.concatenate([total[0:8], total[8:16]], axis=1)
    out_ref[...] = jnp.where(live_rows, result, 0.0).astype(BF16)

    for copy in sends:
        copy.wait_send()


def local(sectors, ny, nz, trial, block_rows, right_ops, left_ops, ent_source, ent_target, ent_count):
    entries, block_len = left_ops.shape[1:3]
    columns = trial.shape[1]
    chips = ny * nz
    far = ny // 2
    dma = pltpu.SemaphoreType.DMA
    vmem = pl.BlockSpec(memory_space=pltpu.VMEM)
    hbm = pl.BlockSpec(memory_space=pl.ANY)
    return pl.pallas_call(
        functools.partial(kernel, sectors, ny, nz),
        out_shape=jax.ShapeDtypeStruct(trial.shape, trial.dtype),
        in_specs=[hbm] * 7,
        out_specs=vmem,
        scratch_shapes=[
            pltpu.VMEM(trial.shape, trial.dtype),
            pltpu.SMEM(block_rows.shape, jnp.int32),
            pltpu.SMEM(ent_source.shape, jnp.int32),
            pltpu.SMEM(ent_target.shape, jnp.int32),
            pltpu.SMEM((1, 1), jnp.int32),
            pltpu.VMEM((2, 2, ny, nz, 16, columns // 2), BF16),
            pltpu.VMEM((4 * block_len, columns), BF16),
            pltpu.VMEM((entries, block_len, block_len), BF16),
            pltpu.VMEM((2, block_len, 4 * block_len), BF16),
            pltpu.VMEM((block_len, 4 * block_len), BF16),
            pltpu.VMEM((columns, columns), BF16),
            pltpu.VMEM((columns, columns), BF16),
            pltpu.VMEM((block_len, 2 * columns), BF16),
            pltpu.VMEM((chips, 16, columns // 2), BF16),
            pltpu.VMEM((5 * nz, 16, columns // 2), BF16),
            pltpu.VMEM((2, nz, 16, columns // 2), BF16),
            pltpu.VMEM((2, nz // 2, 16, columns // 2), BF16),
            dma((7,)), dma((2,)), dma((2,)), dma((nz,)), dma((nz,)),
            dma((nz - 1,)), dma((nz - 1,)),
            dma((2, 2, far)), dma((2, 2, far)),
            dma((2, 2 * far + 1)), dma((2, 2 * far + 1)),
            dma((2, 2)), dma((2, 2)),
            dma((5 * nz,)), dma((5 * nz,)),
        ],
        compiler_params=pltpu.CompilerParams(
            collective_id=0, has_side_effects=True, vmem_limit_bytes=64 * 1024 * 1024,
        ),
        name="sigma",
    )(trial, block_rows, right_ops, left_ops, ent_source, ent_target, ent_count.reshape(1, 1))


def solution(mesh):
    nz = 4
    sectors = mesh.shape["sector"]
    ny = mesh.shape["term"] // (2 * nz)
    placed = (
        P(("sector", "term"), None),
        P("sector"),
        P(("sector", "term"), None, None),
        P(("sector", "term"), None, None, None),
        P(("sector", "term"), None),
        P(("sector", "term"), None),
        P(("sector", "term")),
    )
    return jax.shard_map(
        functools.partial(local, sectors, ny, nz), mesh=mesh, in_specs=placed,
        out_specs=P(("sector", "term"), None), check_vma=False,
    )
```

time: 70.3 us -> 56.1 us (0.80)
  Pallas kernels: 63.3 us -> 53.8 us
  local copies, waits for them, and re-layouts: 6.1 us -> 1.32 us
    pallas_call x1, Pallas kernels: 63.3 us -> 53.8 us  [local(): pl.pallas_call(functools.partial(kernel, sectors, ny, nz), out_shape=jax....]
    unnamed x13 -> x1, local copies, waits for them, and re-layouts: 6.1 us -> 1.32 us
where the time goes in v2:
time: 56.1 us; the launch traced here: 55.8 us
  Pallas kernels  53.8 us (96%)
  local copies, waits for them, and re-layouts  1.32 us (2%)
  between operations  0.66 us (1%)
    pallas_call x1, Pallas kernels, local(): pl.pallas_call(functools.partial(kernel, sectors, ny, nz), out_shape=jax....  53.8 us
    unnamed x1, local copies, waits for them, and re-layouts  1.32 us

profile of v2, /device:TPU:1, one launch (start us, length us, event | category | flops | bytes accessed | tf_op | source)
XLA Modules:
  0.0 55.8 jit_solution(3232943478347729793)
XLA Ops:
  0.7 53.8 %sigma.1 = bf16[8,1024]{1,0:T(8,128)(2,1)} custom-call(bf16[8,1024]{1,0:T(8,128)(2,1)} %trial_in.1, s32[2]{0:T(128)} %rows_in.1, bf16[1,1024,1024]{2,1,0:T(8,128)(2,1)} %right_ref.1, bf16[1,8,256,256]{3,2,1,0:T(8,128)(2,1)} %left_ref.1, s32[1,8]{1,0:T(1,128)} %source_in.1, s32[1,8]{1,0:T(1,128)} %target_in.1, s32[1,1]{1,0:T(1,128)} %bitcast.1.count_in), custom_call_target="tpu_custom_call" | custom-call | tf_op jit(solution)/shard_map/sigma/pallas_call | solution.py:282
  54.4 1.3 %copy.10 = bf16[8,1024]{1,0:T(8,128)(2,1)} copy(bf16[8,1024]{1,0:T(8,128)(2,1)} %sigma.1) | data formatting | bytes 32768

commit v3 on v2

v3 whole, which is shorter than its diff:
```python
import functools

import jax
import jax.numpy as jnp
from jax import lax
from jax.experimental import pallas as pl
from jax.experimental.pallas import tpu as pltpu
from jax.sharding import PartitionSpec as P

MESH = pl.DeviceIdType.MESH
F32 = jnp.float32
BF16 = jnp.bfloat16
SKIP = True


def kernel(
    sectors, ny, nz,
    trial_in, rows_in, right_ref, left_ref, source_in, target_in, count_in,
    out_ref,
    trial_ref, rows_ref, source_ref, target_ref, count_ref,
    units, window, lefts, weights, weights_sib, right_own, right_sib, projected, outgoing, incoming,
    passed, passed_half, early,
    load_sem, pair_send, pair_recv, next_send, next_recv, o_send, o_recv, z_send, z_recv, y_send, y_recv,
    d_send, d_recv, m_send, m_recv, r_send, r_recv,
):
    entries, block_len = lefts.shape[0], lefts.shape[1]
    columns = right_own.shape[0]
    half = columns // 2
    group_rows = 2 * block_len
    chips = ny * nz
    far = ny // 2
    s = lax.axis_index("sector")
    t = lax.axis_index("term")
    y, z, c = t // (2 * nz), lax.rem(t // 2, nz), lax.rem(t, 2)
    me = t // 2

    def device(sector, chip, core):
        return (sector, chip * 2 + core)

    sibling = device(s, me, 1 - c)
    following = lax.rem(s + 1, sectors)
    preceding = lax.rem(s + sectors - 1, sectors)

    def near(dy, dz):
        return lax.rem(y + dy + ny, ny) * nz + lax.rem(z + dz, nz)


    loads = [
        pltpu.make_async_copy(source, destination, load_sem.at[i])
        for i, (source, destination) in enumerate([
            (trial_in, trial_ref), (rows_in, rows_ref), (source_in, source_ref), (target_in, target_ref),
            (count_in, count_ref), (left_ref.at[0], lefts), (right_ref.at[0], right_own),
        ])
    ]
    for load in loads:
        load.start()

    barrier = pltpu.get_barrier_semaphore()

    def greet(target):
        pl.semaphore_signal(barrier, inc=1, device_id=target, device_id_type=MESH)

    greet(sibling)
    for dz in range(nz):
        greet(device(preceding, near(0, dz), c))
    for dy in range(-2, 3):
        for dz in range(nz):
            if dy or dz:
                greet(device(s, near(dy, dz), c))

    loads[0].wait()
    loads[1].wait()
    start_row = t * 8
    limit = rows_ref[start_row // block_len]
    inside = lax.rem(start_row, block_len) + lax.broadcasted_iota(jnp.int32, (8, columns), 0)
    live_rows = inside < limit
    rows = jnp.where(live_rows, trial_ref[...].astype(F32), 0.0)
    units[0, c, y, z] = jnp.concatenate([rows[:, :half], rows[:, half:]], axis=0).astype(BF16)

    pl.semaphore_wait(barrier, 1 + nz + 5 * nz - 1)

    def remote(source, destination, send, recv, target):
        return pltpu.make_async_remote_copy(
            src_ref=source, dst_ref=destination, send_sem=send, recv_sem=recv,
            device_id=target, device_id_type=MESH,
        )

    sends = []

    def begin(copy):
        copy.start()
        sends.append(copy)
        return copy

    def behind(way, k):
        return lax.rem(y - k + ny, ny) if way == 0 else lax.rem(y + k, ny)

    def toward(way, hops):
        return device(s, near(hops if way == 0 else -hops, 0), c)

    def own_unit(way, k):
        if k < far:
            return units.at[0, c, behind(way, k), z]
        return units.at[0, c, behind(way, k), z, :, pl.ds(way * (half // 2), half // 2)]

    def index(way, k):
        return way * far + k if k else 0

    def own_step(way, k, hops):
        row = behind(way, k - hops)
        slot = units.at[0, c, row, z] if k < far else units.at[0, c, row, z, :, pl.ds(way * (half // 2), half // 2)]
        return remote(slot, slot, o_send.at[way, k - 1], o_recv.at[way, k - 1], toward(way, hops))

    def own_spread(way, k):
        slot = own_unit(way, k)
        return [
            remote(slot, slot, z_send.at[index(way, k), d - 1], z_recv.at[index(way, k), d - 1], device(s, near(0, d), c))
            for d in range(nz - 1, 0, -1)
        ]

    def prior_unit(way, k, d):
        return units.at[1, c, behind(way, k), lax.rem(z - d + nz, nz)]

    def carried(way, k):
        return range(nz) if k < far else range(way * (nz // 2), (way + 1) * (nz // 2))

    def prior_step(way, k, d, hops):
        slot = prior_unit(way, k - hops, d)
        return remote(slot, slot, y_send.at[way, k - 1, d], y_recv.at[way, k - 1, d], toward(way, hops))

    def pair_copy(st, way, k, d=None):
        slot = units.at[st, c, behind(way, k)] if d is None else prior_unit(way, k, d)
        at = index(way, k) if d is None else 2 * far + 1 + d
        return remote(slot, slot, d_send.at[st, at], d_recv.at[st, at], sibling)

    own, prior, spread = {}, {}, {}
    for way in range(2):
        own[way, 2] = begin(own_step(way, 2, 2))
        own[way, 1] = begin(own_step(way, 1, 1))
    next_all = [
        begin(remote(units.at[0, c, y, z], units.at[1, c, y, z], next_send.at[d], next_recv.at[d],
                     device(following, near(0, d), c)))
        for d in range(nz)
    ]
    spread[0, 0] = [begin(copy) for copy in own_spread(0, 0)]
    right_copy = begin(remote(right_ref.at[0], right_sib, pair_send.at[1], pair_recv.at[1], sibling))

    pairs = []

    def begin_pair(st, way, k, d=None):
        pairs.append((st, begin(pair_copy(st, way, k, d))))

    def own_arrival(k):
        for way in range(2):
            own[way, k].wait_recv()
            if k == 2:
                own[way, 3] = begin(own_step(way, 3, 1))
                own[way, far] = begin(own_step(way, far, 2))
            spread[way, k] = [begin(copy) for copy in own_spread(way, k)]

    def own_row(k):
        for way in range(2 if k else 1):
            for copy in spread[way, k]:
                copy.wait_recv()
            if k < far:
                begin_pair(0, way, k)
        if k == far:
            begin_pair(0, 0, k)

    def prior_begin(way, k, d, hops):
        if d in carried(way, k):
            prior[way, k, d] = begin(prior_step(way, k, d, hops))

    def prior_arrival(k):
        for d in range(nz):
            for way in range(2):
                if k == 0:
                    if way == 0:
                        next_all[d].wait_recv()
                    if SKIP:
                        prior_begin(way, 2, d, 2)
                    prior_begin(way, 1, d, 1)
                elif d in carried(way, k):
                    prior[way, k, d].wait_recv()
                    if k == 1 and not SKIP:
                        prior_begin(way, 2, d, 1)
                    if k == 2:
                        prior_begin(way, far, d, 2)
                        prior_begin(way, 3, d, 1)
                    if k == far:
                        begin_pair(1, way, k, d)
        if k < far:
            for way in range(2 if k else 1):
                begin_pair(1, way, k)

    own_arrival(1)
    own_arrival(2)
    prior_arrival(0)

    for load in loads[2:6]:
        load.wait()
    count = count_ref[0, 0]
    factors = []
    for k in range(entries):
        live = k < count
        src, dst = source_ref[0, k], target_ref[0, k]
        for b in range(2):
            for w in range(4):
                on = live & (dst == b) & (src == w)
                if w >= 2:
                    on = on & (s > 0)
                factors.append(jnp.where(on, 1.0, 0.0).astype(F32))

    def weigh(i, carry):
        row = pl.multiple_of(i * 32, 32)
        blocks = [lefts[k, pl.ds(row, 32), :].astype(F32) for k in range(entries)]
        at = pl.multiple_of(i * 16, 16)
        for b in range(2):
            for w in range(4):
                total = blocks[0] * factors[b * 4 + w]
                for k in range(1, entries):
                    total = total + blocks[k] * factors[k * 8 + b * 4 + w]
                total = total.reshape(2, 2, 8, block_len)
                for p in range(2):
                    piece = total[:, p].reshape(16, block_len).astype(BF16)
                    weights[p, pl.ds(b * (block_len // 2) + at, 16), w * block_len:(w + 1) * block_len] = piece
        return carry

    lax.fori_loop(0, block_len // 32, weigh, 0)

    weights_copy = begin(remote(weights.at[1 - c], weights_sib, pair_send.at[0], pair_recv.at[0], sibling))

    own_arrival(3)
    own_arrival(4)
    own_row(0)
    prior_arrival(1)
    own_row(1)
    prior_arrival(2)
    own_row(2)
    own_row(3)
    own_row(4)
    prior_arrival(3)
    prior_arrival(4)

    def lay(st):
        def one(row, carry):
            pieces = [units[st, p, row].astype(F32).reshape(nz, 2, 8, half) for p in range(2)]
            at = pl.multiple_of(st * group_rows + row * (nz * 16), 16)
            for h in range(2):
                both = jnp.concatenate([pieces[0][:, h:h + 1], pieces[1][:, h:h + 1]], axis=1)
                window[pl.ds(at, nz * 16), h * half:(h + 1) * half] = both.reshape(nz * 16, half).astype(BF16)
            return carry

        lax.fori_loop(0, ny, one, 0)

    tile = min(256, half)

    def received(st):
        for which, copy in pairs:
            if which == st:
                copy.wait_recv()

    def left_product(operator, st, n):
        rows = slice(st * group_rows, (st + 1) * group_rows)
        return jnp.dot(operator[:, rows], window[rows, n * tile:(n + 1) * tile], preferred_element_type=F32)

    received(0)
    lay(0)
    weights_copy.wait_recv()
    for n in range(columns // tile):
        early[0, :, n * tile:(n + 1) * tile] = left_product(weights[c], 0, n)
        early[1, :, n * tile:(n + 1) * tile] = left_product(weights_sib[...], 0, n)
    received(1)
    lay(1)
    for n in range(columns // tile):
        at = slice(n * tile, (n + 1) * tile)
        projected[:, at] = (early[0, :, at] + left_product(weights[c], 1, n)).astype(BF16)
        at_sib = slice(columns + n * tile, columns + (n + 1) * tile)
        projected[:, at_sib] = (early[1, :, at] + left_product(weights_sib[...], 1, n)).astype(BF16)
    right_copy.wait_recv()
    loads[6].wait()

    def row_at(dy):
        return lax.rem(y + dy + ny, ny) * nz

    part = half // 2
    merged, finals = {}, []

    def deliver(n, dy, dz):
        chip = near(dy, dz)
        at = (2 + dy) * nz
        finals.append(begin(remote(
            outgoing.at[n, chip], incoming.at[n, at + z],
            r_send.at[n, at + dz], r_recv.at[n, at + dz], device(s, chip, c))))

    for n in range(2):
        both = []
        for h in range(2):
            at = h * half + n * part
            value = jnp.dot(projected[:, :columns], right_own[:, at:at + part], preferred_element_type=F32)
            value = value + jnp.dot(projected[:, columns:], right_sib[:, at:at + part], preferred_element_type=F32)
            both.append(value.reshape(chips, 8, part))
        outgoing[n] = jnp.concatenate(both, axis=1).astype(BF16)
        for way, sign in ((0, 1), (1, -1)):
            merged[n, way] = (
                begin(remote(outgoing.at[n, pl.ds(row_at(4) + way * (nz // 2), nz // 2)], passed_half.at[n, way],
                             m_send.at[n, way, 1], m_recv.at[n, way, 1], device(s, near(2 * sign, 0), c))),
                begin(remote(outgoing.at[n, pl.ds(row_at(3 * sign), nz)], passed.at[n, way],
                             m_send.at[n, way, 0], m_recv.at[n, way, 0], device(s, near(sign, 0), c))),
            )

    for n in range(2):
        for dy in (1, -1, 0):
            for dz in range(nz - 1, -1, -1):
                if dy or dz:
                    deliver(n, dy, dz)
        incoming[n, 2 * nz + z] = outgoing[n, me]
    for n in range(2):
        for way, sign in ((0, 1), (1, -1)):
            for copy in merged[n, way]:
                copy.wait_recv()
            for i in range(nz):
                at = row_at(2 * sign) + i
                value = outgoing[n, at].astype(F32) + passed[n, way, i].astype(F32)
                if i // (nz // 2) == way:
                    value = value + passed_half[n, way, i % (nz // 2)].astype(F32)
                outgoing[n, at] = value.astype(BF16)
            for dz in range(nz - 1, -1, -1):
                deliver(n, 2 * sign, dz)

    for copy in finals:
        copy.wait_recv()
    for n in range(2):
        total = incoming[n, 0].astype(F32)
        for i in range(1, 5 * nz):
            total = total + incoming[n, i].astype(F32)
        for h in range(2):
            at = h * half + n * part
            out_ref[:, at:at + part] = jnp.where(
                live_rows[:, :part], total[h * 8:(h + 1) * 8], 0.0).astype(BF16)

    for copy in sends:
        copy.wait_send()


def local(sectors, ny, nz, trial, block_rows, right_ops, left_ops, ent_source, ent_target, ent_count):
    entries, block_len = left_ops.shape[1:3]
    columns = trial.shape[1]
    chips = ny * nz
    far = ny // 2
    dma = pltpu.SemaphoreType.DMA
    vmem = pl.BlockSpec(memory_space=pltpu.VMEM)
    hbm = pl.BlockSpec(memory_space=pl.ANY)
    return pl.pallas_call(
        functools.partial(kernel, sectors, ny, nz),
        out_shape=jax.ShapeDtypeStruct(trial.shape, trial.dtype),
        in_specs=[hbm] * 7,
        out_specs=vmem,
        scratch_shapes=[
            pltpu.VMEM(trial.shape, trial.dtype),
            pltpu.SMEM(block_rows.shape, jnp.int32),
            pltpu.SMEM(ent_source.shape, jnp.int32),
            pltpu.SMEM(ent_target.shape, jnp.int32),
            pltpu.SMEM((1, 1), jnp.int32),
            pltpu.VMEM((2, 2, ny, nz, 16, columns // 2), BF16),
            pltpu.VMEM((4 * block_len, columns), BF16),
            pltpu.VMEM((entries, block_len, block_len), BF16),
            pltpu.VMEM((2, block_len, 4 * block_len), BF16),
            pltpu.VMEM((block_len, 4 * block_len), BF16),
            pltpu.VMEM((columns, columns), BF16),
            pltpu.VMEM((columns, columns), BF16),
            pltpu.VMEM((block_len, 2 * columns), BF16),
            pltpu.VMEM((2, chips, 16, columns // 4), BF16),
            pltpu.VMEM((2, 5 * nz, 16, columns // 4), BF16),
            pltpu.VMEM((2, 2, nz, 16, columns // 4), BF16),
            pltpu.VMEM((2, 2, nz // 2, 16, columns // 4), BF16),
            pltpu.VMEM((2, block_len, columns), F32),
            dma((7,)), dma((2,)), dma((2,)), dma((nz,)), dma((nz,)),
            dma((2, far)), dma((2, far)),
            dma((2 * far + 1, nz - 1)), dma((2 * far + 1, nz - 1)),
            dma((2, far, nz)), dma((2, far, nz)),
            dma((2, 2 * far + 1 + nz)), dma((2, 2 * far + 1 + nz)),
            dma((2, 2, 2)), dma((2, 2, 2)),
            dma((2, 5 * nz)), dma((2, 5 * nz)),
        ],
        compiler_params=pltpu.CompilerParams(
            collective_id=0, has_side_effects=True, vmem_limit_bytes=64 * 1024 * 1024,
        ),
        name="sigma",
    )(trial, block_rows, right_ops, left_ops, ent_source, ent_target, ent_count.reshape(1, 1))


def solution(mesh):
    nz = 4
    sectors = mesh.shape["sector"]
    ny = mesh.shape["term"] // (2 * nz)
    placed = (
        P(("sector", "term"), None),
        P("sector"),
        P(("sector", "term"), None, None),
        P(("sector", "term"), None, None, None),
        P(("sector", "term"), None),
        P(("sector", "term"), None),
        P(("sector", "term")),
    )
    return jax.shard_map(
        functools.partial(local, sectors, ny, nz), mesh=mesh, in_specs=placed,
        out_specs=P(("sector", "term"), None), check_vma=False,
    )
```

time: 56.1 us -> 50.3 us (0.90)
  Pallas kernels: 53.8 us -> 48 us
    pallas_call x1, Pallas kernels: 53.8 us -> 48 us  [local(): pl.pallas_call(functools.partial(kernel, sectors, ny, nz), out_shape=jax....]
where the time goes in v3:
time: 50.3 us; the launch traced here: 50 us
  Pallas kernels  48 us (95%)
  local copies, waits for them, and re-layouts  1.32 us (3%)
  between operations  0.66 us (1%)
    pallas_call x1, Pallas kernels, local(): pl.pallas_call(functools.partial(kernel, sectors, ny, nz), out_shape=jax....  48 us
    unnamed x1, local copies, waits for them, and re-layouts  1.32 us

profile of v3, /device:TPU:1, one launch (start us, length us, event | category | flops | bytes accessed | tf_op | source)
XLA Modules:
  0.0 50.0 jit_solution(9219176776643102855)
XLA Ops:
  0.7 48.0 %sigma.1 = bf16[8,1024]{1,0:T(8,128)(2,1)} custom-call(bf16[8,1024]{1,0:T(8,128)(2,1)} %trial_in.1, s32[2]{0:T(128)} %rows_in.1, bf16[1,1024,1024]{2,1,0:T(8,128)(2,1)} %right_ref.1, bf16[1,8,256,256]{3,2,1,0:T(8,128)(2,1)} %left_ref.1, s32[1,8]{1,0:T(1,128)} %source_in.1, s32[1,8]{1,0:T(1,128)} %target_in.1, s32[1,1]{1,0:T(1,128)} %bitcast.1.count_in), custom_call_target="tpu_custom_call" | custom-call | tf_op jit(solution)/shard_map/sigma/pallas_call | solution.py:354
  48.7 1.3 %copy.10 = bf16[8,1024]{1,0:T(8,128)(2,1)} copy(bf16[8,1024]{1,0:T(8,128)(2,1)} %sigma.1) | data formatting | bytes 32768

commit v4 on v3

--- a/solution.py
+++ b/solution.py
@@ -10,7 +10,6 @@
 MESH = pl.DeviceIdType.MESH
 F32 = jnp.float32
 BF16 = jnp.bfloat16
-SKIP = True
 
 
 def kernel(
@@ -61,8 +60,12 @@
         pl.semaphore_signal(barrier, inc=1, device_id=target, device_id_type=MESH)
 
     greet(sibling)
-    for dz in range(nz):
-        greet(device(preceding, near(0, dz), c))
+
+    @pl.when(s > 0)
+    def _():
+        for dz in range(nz):
+            greet(device(preceding, near(0, dz), c))
+
     for dy in range(-2, 3):
         for dz in range(nz):
             if dy or dz:
@@ -77,7 +80,14 @@
     rows = jnp.where(live_rows, trial_ref[...].astype(F32), 0.0)
     units[0, c, y, z] = jnp.concatenate([rows[:, :half], rows[:, half:]], axis=0).astype(BF16)
 
-    pl.semaphore_wait(barrier, 1 + nz + 5 * nz - 1)
+    @pl.when(s < sectors - 1)
+    def _():
+        pl.semaphore_wait(barrier, 6 * nz)
+
+    @pl.when(s == sectors - 1)
+    def _():
+        pl.semaphore_wait(barrier, 5 * nz)
+
 
     def remote(source, destination, send, recv, target):
         return pltpu.make_async_remote_copy(
@@ -133,22 +143,38 @@
         at = index(way, k) if d is None else 2 * far + 1 + d
         return remote(slot, slot, d_send.at[st, at], d_recv.at[st, at], sibling)
 
-    own, prior, spread = {}, {}, {}
+    own, spread = {}, {}
     for way in range(2):
         own[way, 2] = begin(own_step(way, 2, 2))
         own[way, 1] = begin(own_step(way, 1, 1))
     next_all = [
-        begin(remote(units.at[0, c, y, z], units.at[1, c, y, z], next_send.at[d], next_recv.at[d],
-                     device(following, near(0, d), c)))
+        remote(units.at[0, c, y, z], units.at[1, c, y, z], next_send.at[d], next_recv.at[d],
+               device(following, near(0, d), c))
         for d in range(nz)
     ]
+
+    @pl.when(s < sectors - 1)
+    def _():
+        for copy in next_all:
+            copy.start()
+
     spread[0, 0] = [begin(copy) for copy in own_spread(0, 0)]
-    right_copy = begin(remote(right_ref.at[0], right_sib, pair_send.at[1], pair_recv.at[1], sibling))
 
     pairs = []
 
-    def begin_pair(st, way, k, d=None):
-        pairs.append((st, begin(pair_copy(st, way, k, d))))
+    prior = {
+        (way, k, d): prior_step(way, k, d, 2 if k in (2, far) else 1)
+        for k in range(1, far + 1) for way in range(2) for d in carried(way, k)
+    }
+    prior_pairs = {(0, 0): [pair_copy(1, 0, 0)]}
+    for k in range(1, far):
+        for way in range(2):
+            prior_pairs[way, k] = [pair_copy(1, way, k)]
+    for way in range(2):
+        prior_pairs[way, far] = [pair_copy(1, way, far, d) for d in carried(way, far)]
+
+    def begin_pair(way, k):
+        pairs.append(begin(pair_copy(0, way, k)))
 
     def own_arrival(k):
         for way in range(2):
@@ -163,35 +189,31 @@
             for copy in spread[way, k]:
                 copy.wait_recv()
             if k < far:
-                begin_pair(0, way, k)
+                begin_pair(way, k)
         if k == far:
-            begin_pair(0, 0, k)
-
-    def prior_begin(way, k, d, hops):
-        if d in carried(way, k):
-            prior[way, k, d] = begin(prior_step(way, k, d, hops))
+            begin_pair(0, k)
 
     def prior_arrival(k):
-        for d in range(nz):
-            for way in range(2):
+        @pl.when(s > 0)
+        def _():
+            for d in range(nz):
                 if k == 0:
-                    if way == 0:
-                        next_all[d].wait_recv()
-                    if SKIP:
-                        prior_begin(way, 2, d, 2)
-                    prior_begin(way, 1, d, 1)
-                elif d in carried(way, k):
-                    prior[way, k, d].wait_recv()
-                    if k == 1 and not SKIP:
-                        prior_begin(way, 2, d, 1)
-                    if k == 2:
-                        prior_begin(way, far, d, 2)
-                        prior_begin(way, 3, d, 1)
-                    if k == far:
-                        begin_pair(1, way, k, d)
-        if k < far:
-            for way in range(2 if k else 1):
-                begin_pair(1, way, k)
+                    next_all[d].wait_recv()
+                for way in range(2):
+                    if k == 0:
+                        prior[way, 2, d].start()
+                        prior[way, 1, d].start()
+                    elif d in carried(way, k):
+                        prior[way, k, d].wait_recv()
+                        if k == 2:
+                            if d in carried(way, far):
+                                prior[way, far, d].start()
+                            prior[way, 3, d].start()
+                        if k == far:
+                            prior_pairs[way, far][d - carried(way, far)[0]].start()
+            if k < far:
+                for way in range(2 if k else 1):
+                    prior_pairs[way, k][0].start()
 
     own_arrival(1)
     own_arrival(2)
@@ -228,6 +250,7 @@
 
     lax.fori_loop(0, block_len // 32, weigh, 0)
 
+    right_copy = begin(remote(right_ref.at[0], right_sib, pair_send.at[1], pair_recv.at[1], sibling))
     weights_copy = begin(remote(weights.at[1 - c], weights_sib, pair_send.at[0], pair_recv.at[0], sibling))
 
     own_arrival(3)
@@ -255,23 +278,29 @@
 
     tile = min(256, half)
 
-    def received(st):
-        for which, copy in pairs:
-            if which == st:
-                copy.wait_recv()
-
     def left_product(operator, st, n):
         rows = slice(st * group_rows, (st + 1) * group_rows)
         return jnp.dot(operator[:, rows], window[rows, n * tile:(n + 1) * tile], preferred_element_type=F32)
 
-    received(0)
+    for copy in pairs:
+        copy.wait_recv()
     lay(0)
     weights_copy.wait_recv()
     for n in range(columns // tile):
         early[0, :, n * tile:(n + 1) * tile] = left_product(weights[c], 0, n)
         early[1, :, n * tile:(n + 1) * tile] = left_product(weights_sib[...], 0, n)
-    received(1)
-    lay(1)
+
+    @pl.when(s > 0)
+    def _():
+        for copies in prior_pairs.values():
+            for copy in copies:
+                copy.wait_recv()
+        lay(1)
+
+    @pl.when(s == 0)
+    def _():
+        window[group_rows:, :] = jnp.zeros((group_rows, columns), BF16)
+
     for n in range(columns // tile):
         at = slice(n * tile, (n + 1) * tile)
         projected[:, at] = (early[0, :, at] + left_product(weights[c], 1, n)).astype(BF16)
@@ -328,6 +357,23 @@
             for dz in range(nz - 1, -1, -1):
                 deliver(n, 2 * sign, dz)
 
+    early_sends = len(sends) - 4 * nz
+    for copy in sends[:early_sends]:
+        copy.wait_send()
+
+    @pl.when(s > 0)
+    def _():
+        for copy in prior.values():
+            copy.wait_send()
+        for copies in prior_pairs.values():
+            for copy in copies:
+                copy.wait_send()
+
+    @pl.when(s < sectors - 1)
+    def _():
+        for copy in next_all:
+            copy.wait_send()
+
     for copy in finals:
         copy.wait_recv()
     for n in range(2):
@@ -339,7 +385,7 @@
             out_ref[:, at:at + part] = jnp.where(
                 live_rows[:, :part], total[h * 8:(h + 1) * 8], 0.0).astype(BF16)
 
-    for copy in sends:
+    for copy in sends[early_sends:]:
         copy.wait_send()
 
 

time: 50.3 us -> 47.7 us (0.948)
  the two profiles are of different devices: /device:TPU:1 before, /device:TPU:6 now
where the time goes in v4:
time: 47.7 us; the launch traced here: 47.4 us
  Pallas kernels  45.4 us (95%)
  local copies, waits for them, and re-layouts  1.32 us (3%)
  between operations  0.66 us (1%)
    pallas_call x1, Pallas kernels, local(): pl.pallas_call(functools.partial(kernel, sectors, ny, nz), out_shape=jax....  45.4 us
    unnamed x1, local copies, waits for them, and re-layouts  1.32 us

profile of v4, /device:TPU:6, one launch (start us, length us, event | category | flops | bytes accessed | tf_op | source)
XLA Modules:
  0.0 47.4 jit_solution(18364556585168507646)
XLA Ops:
  0.7 45.4 %sigma.1 = bf16[8,1024]{1,0:T(8,128)(2,1)} custom-call(bf16[8,1024]{1,0:T(8,128)(2,1)} %trial_in.1, s32[2]{0:T(128)} %rows_in.1, bf16[1,1024,1024]{2,1,0:T(8,128)(2,1)} %right_ref.1, bf16[1,8,256,256]{3,2,1,0:T(8,128)(2,1)} %left_ref.1, s32[1,8]{1,0:T(1,128)} %source_in.1, s32[1,8]{1,0:T(1,128)} %target_in.1, s32[1,1]{1,0:T(1,128)} %bitcast.1.count_in), custom_call_target="tpu_custom_call" | custom-call | tf_op jit(solution)/shard_map/sigma/pallas_call | solution.py:400
  46.0 1.3 %copy.10 = bf16[8,1024]{1,0:T(8,128)(2,1)} copy(bf16[8,1024]{1,0:T(8,128)(2,1)} %sigma.1) | data formatting | bytes 32768

commit v5 on v4

--- a/solution.py
+++ b/solution.py
@@ -399,7 +399,7 @@
     hbm = pl.BlockSpec(memory_space=pl.ANY)
     return pl.pallas_call(
         functools.partial(kernel, sectors, ny, nz),
-        out_shape=jax.ShapeDtypeStruct(trial.shape, trial.dtype),
+        out_shape=pltpu.VMEM(trial.shape, trial.dtype),
         in_specs=[hbm] * 7,
         out_specs=vmem,
         scratch_shapes=[
@@ -430,7 +430,7 @@
             dma((2, 5 * nz)), dma((2, 5 * nz)),
         ],
         compiler_params=pltpu.CompilerParams(
-            collective_id=0, has_side_effects=True, vmem_limit_bytes=64 * 1024 * 1024,
+            collective_id=0, has_side_effects=True, vmem_limit_bytes=56 * 1024 * 1024,
         ),
         name="sigma",
     )(trial, block_rows, right_ops, left_ops, ent_source, ent_target, ent_count.reshape(1, 1))

time: 47.7 us -> 46.2 us (0.969)
  local copies, waits for them, and re-layouts: 1.32 us -> 0.61 us
  Pallas kernels: 45.4 us -> 44.8 us
    unnamed x1, local copies, waits for them, and re-layouts: 1.32 us -> 0.61 us
    pallas_call x1, Pallas kernels: 45.4 us -> 44.8 us  [local(): pl.pallas_call(functools.partial(kernel, sectors, ny, nz), out_shape=pltp...]
where the time goes in v5:
time: 46.2 us; the launch traced here: 46 us
  Pallas kernels  44.8 us (97%)
  between operations  0.66 us (1%)
  local copies, waits for them, and re-layouts  0.61 us (1%)
    pallas_call x1, Pallas kernels, local(): pl.pallas_call(functools.partial(kernel, sectors, ny, nz), out_shape=pltp...  44.8 us

profile of v5, /device:TPU:6, one launch (start us, length us, event | category | flops | bytes accessed | tf_op | source)
XLA Modules:
  0.0 46.0 jit_solution(12953178587492332682)
XLA Ops:
  0.7 44.8 %sigma.1 = bf16[8,1024]{1,0:T(8,128)(2,1)S(1)} custom-call(bf16[8,1024]{1,0:T(8,128)(2,1)} %trial_in.1, s32[2]{0:T(128)} %rows_in.1, bf16[1,1024,1024]{2,1,0:T(8,128)(2,1)} %right_ref.1, bf16[1,8,256,256]{3,2,1,0:T(8,128)(2,1)} %left_ref.1, s32[1,8]{1,0:T(1,128)} %source_in.1, s32[1,8]{1,0:T(1,128)} %target_in.1, s32[1,1]{1,0:T(1,128)} %bitcast.1.count_in), custom_call_target="tpu_custom_call" | custom-call | tf_op jit(solution)/shard_map/sigma/pallas_call | solution.py:400
  45.4 0.6 %copy.9 = bf16[8,1024]{1,0:T(8,128)(2,1)} copy(bf16[8,1024]{1,0:T(8,128)(2,1)S(1)} %sigma.1) | data formatting | bytes 32768

commit v6 on v5

--- a/solution.py
+++ b/solution.py
@@ -17,7 +17,7 @@
     trial_in, rows_in, right_ref, left_ref, source_in, target_in, count_in,
     out_ref,
     trial_ref, rows_ref, source_ref, target_ref, count_ref,
-    units, window, lefts, weights, weights_sib, right_own, right_sib, projected, outgoing, incoming,
+    units, window, lefts, weights, stacked, right_own, right_sib, projected, outgoing, incoming,
     passed, passed_half, early,
     load_sem, pair_send, pair_recv, next_send, next_recv, o_send, o_recv, z_send, z_recv, y_send, y_recv,
     d_send, d_recv, m_send, m_recv, r_send, r_recv,
@@ -68,7 +68,7 @@
 
     for dy in range(-2, 3):
         for dz in range(nz):
-            if dy or dz:
+            if (dy == 0) != (dz == 0):
                 greet(device(s, near(dy, dz), c))
 
     loads[0].wait()
@@ -82,11 +82,11 @@
 
     @pl.when(s < sectors - 1)
     def _():
-        pl.semaphore_wait(barrier, 6 * nz)
+        pl.semaphore_wait(barrier, 2 * nz + 4)
 
     @pl.when(s == sectors - 1)
     def _():
-        pl.semaphore_wait(barrier, 5 * nz)
+        pl.semaphore_wait(barrier, nz + 4)
 
 
     def remote(source, destination, send, recv, target):
@@ -251,7 +251,10 @@
     lax.fori_loop(0, block_len // 32, weigh, 0)
 
     right_copy = begin(remote(right_ref.at[0], right_sib, pair_send.at[1], pair_recv.at[1], sibling))
-    weights_copy = begin(remote(weights.at[1 - c], weights_sib, pair_send.at[0], pair_recv.at[0], sibling))
+    weights_copy = begin(remote(weights.at[1 - c], stacked.at[pl.ds(block_len, block_len)],
+                                pair_send.at[0], pair_recv.at[0], sibling))
+    keep = pltpu.make_async_copy(weights.at[c], stacked.at[pl.ds(0, block_len)], load_sem.at[7])
+    keep.start()
 
     own_arrival(3)
     own_arrival(4)
@@ -278,17 +281,17 @@
 
     tile = min(256, half)
 
-    def left_product(operator, st, n):
+    def left_product(st, n):
         rows = slice(st * group_rows, (st + 1) * group_rows)
-        return jnp.dot(operator[:, rows], window[rows, n * tile:(n + 1) * tile], preferred_element_type=F32)
+        return jnp.dot(stacked[:, rows], window[rows, n * tile:(n + 1) * tile], preferred_element_type=F32)
 
     for copy in pairs:
         copy.wait_recv()
     lay(0)
     weights_copy.wait_recv()
+    keep.wait()
     for n in range(columns // tile):
-        early[0, :, n * tile:(n + 1) * tile] = left_product(weights[c], 0, n)
-        early[1, :, n * tile:(n + 1) * tile] = left_product(weights_sib[...], 0, n)
+        early[:, n * tile:(n + 1) * tile] = left_product(0, n)
 
     @pl.when(s > 0)
     def _():
@@ -303,9 +306,9 @@
 
     for n in range(columns // tile):
         at = slice(n * tile, (n + 1) * tile)
-        projected[:, at] = (early[0, :, at] + left_product(weights[c], 1, n)).astype(BF16)
-        at_sib = slice(columns + n * tile, columns + (n + 1) * tile)
-        projected[:, at_sib] = (early[1, :, at] + left_product(weights_sib[...], 1, n)).astype(BF16)
+        value = (early[:, at] + left_product(1, n)).astype(BF16)
+        projected[:, at] = value[:block_len]
+        projected[:, columns + n * tile:columns + (n + 1) * tile] = value[block_len:]
     right_copy.wait_recv()
     loads[6].wait()
 
@@ -412,7 +415,7 @@
             pltpu.VMEM((4 * block_len, columns), BF16),
             pltpu.VMEM((entries, block_len, block_len), BF16),
             pltpu.VMEM((2, block_len, 4 * block_len), BF16),
-            pltpu.VMEM((block_len, 4 * block_len), BF16),
+            pltpu.VMEM((2 * block_len, 4 * block_len), BF16),
             pltpu.VMEM((columns, columns), BF16),
             pltpu.VMEM((columns, columns), BF16),
             pltpu.VMEM((block_len, 2 * columns), BF16),
@@ -420,8 +423,8 @@
             pltpu.VMEM((2, 5 * nz, 16, columns // 4), BF16),
             pltpu.VMEM((2, 2, nz, 16, columns // 4), BF16),
             pltpu.VMEM((2, 2, nz // 2, 16, columns // 4), BF16),
-            pltpu.VMEM((2, block_len, columns), F32),
-            dma((7,)), dma((2,)), dma((2,)), dma((nz,)), dma((nz,)),
+            pltpu.VMEM((2 * block_len, columns), F32),
+            dma((8,)), dma((2,)), dma((2,)), dma((nz,)), dma((nz,)),
             dma((2, far)), dma((2, far)),
             dma((2 * far + 1, nz - 1)), dma((2 * far + 1, nz - 1)),
             dma((2, far, nz)), dma((2, far, nz)),

time: 46.2 us -> 46.3 us (level)
  no operation moved by 1% of the time
where the time goes in v6:
time: 46.3 us; the launch traced here: 46.1 us
  Pallas kernels  44.8 us (97%)
  between operations  0.66 us (1%)
  local copies, waits for them, and re-layouts  0.61 us (1%)
    pallas_call x1, Pallas kernels, local(): pl.pallas_call(functools.partial(kernel, sectors, ny, nz), out_shape=pltp...  44.8 us

profile of v6, /device:TPU:6, one launch (start us, length us, event | category | flops | bytes accessed | tf_op | source)
XLA Modules:
  0.0 46.1 jit_solution(16856083789458298241)
XLA Ops:
  0.7 44.8 %sigma.1 = bf16[8,1024]{1,0:T(8,128)(2,1)S(1)} custom-call(bf16[8,1024]{1,0:T(8,128)(2,1)} %trial_in.1, s32[2]{0:T(128)} %rows_in.1, bf16[1,1024,1024]{2,1,0:T(8,128)(2,1)} %right_ref.1, bf16[1,8,256,256]{3,2,1,0:T(8,128)(2,1)} %left_ref.1, s32[1,8]{1,0:T(1,128)} %source_in.1, s32[1,8]{1,0:T(1,128)} %target_in.1, s32[1,1]{1,0:T(1,128)} %bitcast.1.count_in), custom_call_target="tpu_custom_call" | custom-call | tf_op jit(solution)/shard_map/sigma/pallas_call | solution.py:403
  45.5 0.6 %copy.9 = bf16[8,1024]{1,0:T(8,128)(2,1)} copy(bf16[8,1024]{1,0:T(8,128)(2,1)S(1)} %sigma.1) | data formatting | bytes 32768

commit v7 on v6

--- a/solution.py
+++ b/solution.py
@@ -279,7 +279,7 @@
 
         lax.fori_loop(0, ny, one, 0)
 
-    tile = min(256, half)
+    tile = half
 
     def left_product(st, n):
         rows = slice(st * group_rows, (st + 1) * group_rows)

time: 46.3 us -> 46.3 us (level)
  no operation moved by 1% of the time
where the time goes in v7:
time: 46.3 us; the launch traced here: 46.1 us
  Pallas kernels  44.8 us (97%)
  between operations  0.66 us (1%)
  local copies, waits for them, and re-layouts  0.61 us (1%)
    pallas_call x1, Pallas kernels, local(): pl.pallas_call(functools.partial(kernel, sectors, ny, nz), out_shape=pltp...  44.8 us

profile of v7, /device:TPU:6, one launch (start us, length us, event | category | flops | bytes accessed | tf_op | source)
XLA Modules:
  0.0 46.1 jit_solution(16856083789458298241)
XLA Ops:
  0.7 44.8 %sigma.1 = bf16[8,1024]{1,0:T(8,128)(2,1)S(1)} custom-call(bf16[8,1024]{1,0:T(8,128)(2,1)} %trial_in.1, s32[2]{0:T(128)} %rows_in.1, bf16[1,1024,1024]{2,1,0:T(8,128)(2,1)} %right_ref.1, bf16[1,8,256,256]{3,2,1,0:T(8,128)(2,1)} %left_ref.1, s32[1,8]{1,0:T(1,128)} %source_in.1, s32[1,8]{1,0:T(1,128)} %target_in.1, s32[1,1]{1,0:T(1,128)} %bitcast.1.count_in), custom_call_target="tpu_custom_call" | custom-call | tf_op jit(solution)/shard_map/sigma/pallas_call | solution.py:403
  45.5 0.6 %copy.9 = bf16[8,1024]{1,0:T(8,128)(2,1)} copy(bf16[8,1024]{1,0:T(8,128)(2,1)S(1)} %sigma.1) | data formatting | bytes 32768
